TPU v7x, 32 devices: a whole 2x2x4 slice. The times are simulated.
32 devices in a mesh: prow: 8 (over z, x), pcol: 4 (over y, core).
Axes of the slice: x: 2, y: 2, z: 4, core: 2. Of those that a mesh axis runs over, the one named last changes fastest.
Arguments:
- right_hand_blocks: float32 [8, 4, 512, 256], P('prow'), may hold values from -6 to 6
- diag_inverse: bfloat16 [8, 4, 512, 512], P('prow'), as said below
- lower_blocks: bfloat16 [8, 4, 3, 5, 512, 512], P('prow', 'pcol'), may hold values from -0.0625 to 0.0625
- block_source: int32 [8, 4, 3, 5], P('prow', 'pcol'), may hold values from 0 to 1, as said below
- target_level_per_slot: int32 [8, 4, 3, 5], P('prow', 'pcol'), may hold values from 1 to 4, as said below
Outputs:
- solved: bfloat16 [8, 4, 512, 256], P('prow')
Inputs may be any that keep to these rules, and one draw needn't show every extreme that they name: `target_level_per_slot`: block (source k, target level t) appears at most once among the slots of one device and one source level l; every target level exceeds l; the filled slots come first, and there are min(5, 2 * (3 - l)) of them. `block_source`: an empty slot has source 0. `diag_inverse`: lower triangular, diagonal between 0.5 and 1.5.
All inputs are finite; a program needn't handle non-finite values.
Results may differ from a plain program's by a relative error of at most 0.0075.
Values may be sent and summed in bfloat16 or wider, within the bound.
A program may use at most 128 MiB of HBM per device.

v0:
```python
import jax
import jax.numpy as jnp
from jax import lax
from jax.sharding import PartitionSpec as P


def on_device(right_hand_blocks, diag_inverse, lower_blocks, block_source, target_level_per_slot):
    col_count = lax.axis_size("pcol")
    row_count = lax.axis_size("prow")
    per_col = row_count // col_count
    column = lax.axis_index("pcol")
    levels = right_hand_blocks.shape[1]
    block_width = right_hand_blocks.shape[2]
    rhs_cols = right_hand_blocks.shape[3]
    partial_value = jnp.zeros((levels, block_width, rhs_cols), jnp.float32)
    outputs = []
    for tree_level in range(levels):
        inverse = diag_inverse[0, tree_level]
        given_rhs = right_hand_blocks[0, tree_level]
        if tree_level == 0:
            solved = jnp.dot(
                inverse, given_rhs.astype(jnp.bfloat16), preferred_element_type=jnp.float32
            ).astype(jnp.bfloat16)
        else:
            summed = lax.psum(partial_value[tree_level], "pcol")
            solved = jnp.dot(
                inverse,
                (given_rhs - summed).astype(jnp.bfloat16),
                preferred_element_type=jnp.float32,
            ).astype(jnp.bfloat16)
        outputs.append(solved)
        if tree_level < levels - 1:
            gathered = lax.all_gather(solved, "prow", axis=0, tiled=True)
            gathered = gathered.reshape(per_col, col_count, block_width, rhs_cols)
            by_slot = lax.dynamic_index_in_dim(gathered, column, 1, keepdims=False)
            sources = block_source[0, 0, tree_level]
            targets = target_level_per_slot[0, 0, tree_level]
            picked = jnp.take(by_slot, sources, axis=0)
            block_products = jnp.einsum(
                "bij,bjr->bir",
                lower_blocks[0, 0, tree_level],
                picked,
                preferred_element_type=jnp.float32,
            )
            indicator_matrix = (
                targets[None, :] == jnp.arange(levels, dtype=jnp.int32)[:, None]
            ).astype(jnp.float32)
            partial_value = partial_value + jnp.einsum(
                "tk,kxz->txz", indicator_matrix, block_products, precision=lax.Precision.HIGHEST
            )
    return jnp.stack(outputs, axis=0)[None]


def solution(mesh):
    placed = (
        P("prow", None, None, None),
        P("prow", None, None, None),
        P("prow", "pcol", None, None, None, None),
        P("prow", "pcol", None, None),
        P("prow", "pcol", None, None),
    )
    return jax.shard_map(
        on_device,
        mesh=mesh,
        in_specs=placed,
        out_specs=P("prow", None, None, None),
        check_vma=False,
    )
```

profile of v0, /device:TPU:0, one launch (start us, length us, event | category | flops | bytes accessed | tf_op | source)
XLA Modules:
  0.0 322.7 jit_solution(16675195253927854351)
XLA Ops:
  6.5 0.0 all-gather.4.cloned.1.call-start
  6.5 2.2 convolution_convert_fusion.3
  8.8 0.0 all-gather.4.cloned.1.call-update
  8.8 0.0 all-reduce.4.cloned.1.call-start
  8.8 0.7 compare_and_fusion
  9.5 0.7 slice_bitcast_fusion
  10.2 51.3 %all-gather.4.cloned.1.call-done = bf16[4096,256]{1,0:T(8,128)(2,1)} async-done(((bf16[512,256]{1,0:T(8,128)(2,1)}), bf16[4096,256]{1,0:T(8,128)(2,1)}) %all-gather.4.cloned.1.call-update) | async-done | bytes 2097168 | tf_op jit(solution)/shard_map/all_gather | solution.py:33
  61.5 1.1 dynamic-slice_bitcast_fusion.2
  62.6 1.8 gather_fusion
  64.4 3.2 fusion.10
  67.5 3.5 %copy.9 = f32[5,256,512]{1,0,2:T(8,128)} copy(f32[5,256,512]{2,1,0:T(8,128)S(1)} %fusion.10) | data formatting | bytes 5242880 | tf_op jit(solution)/shard_map/bij,bjr->bir/dot_general | solution.py:39
  71.0 4.2 %fusion.4 = f32[4,512,256]{2,0,1:T(4,128)S(1)} fusion(f32[5,256,512]{1,0,2:T(8,128)} %copy.9, s32[5]{0:T(128)S(1)} %get-tuple-element.13), kind=kOutput, calls=%fused_computation.7 | convolution fusion | flops 31457300 | bytes 4718612 | tf_op jit(solution)/shard_map/tk,kxz->txz/dot_general | solution.py:48
  75.3 0.5 slice.88
  75.8 0.8 copy.23
  76.7 0.0 all-reduce.4.cloned.1.call-update
  76.7 0.0 all-gather.6.cloned.1.call-start
  76.7 31.8 %all-reduce.4.cloned.1.call-done = f32[512,256]{1,0:T(8,128)} async-done(((f32[512,256]{1,0:T(8,128)}), f32[512,256]{1,0:T(8,128)}) %all-reduce.4.cloned.1.call-update) | async-done | bytes 524304 | tf_op jit(solution)/shard_map/psum | solution.py:25
  108.5 2.4 convolution_convert_fusion.2
  110.9 0.0 all-gather.6.cloned.1.call-update
  110.9 0.0 all-reduce.6.cloned.1.call-start
  111.0 49.4 %all-gather.6.cloned.1.call-done = bf16[4096,256]{1,0:T(8,128)(2,1)} async-done(((bf16[512,256]{1,0:T(8,128)(2,1)}), bf16[4096,256]{1,0:T(8,128)(2,1)}) %all-gather.6.cloned.1.call-update) | async-done | bytes 2097168 | tf_op jit(solution)/shard_map/all_gather | solution.py:33
  160.4 1.1 dynamic-slice_bitcast_fusion.1
  161.4 1.8 gather_fusion.1
  163.2 4.7 %fusion.8 = f32[5,256,512]{2,1,0:T(8,128)} fusion(bf16[1,1,3,5,512,512]{5,4,3,2,1,0:T(8,128)(2,1)} %param.9, bf16[5,512,256]{2,1,0:T(8,128)(2,1)} %gather_fusion.1, pred[5]{0:T(512)(128)(4,1)S(1)} %get-tuple-element.17), kind=kOutput, calls=%fused_computation.11 | convolution fusion | flops 671744000 | bytes 6553605 | tf_op jit(solution)/shard_map/bij,bjr->bir/dot_general | solution.py:39
  167.9 5.0 %copy.11 = f32[5,256,512]{1,0,2:T(8,128)} copy(f32[5,256,512]{2,1,0:T(8,128)} %fusion.8) | data formatting | bytes 5242880 | tf_op jit(solution)/shard_map/bij,bjr->bir/dot_general | solution.py:39
  172.9 4.4 %fusion.15 = f32[4,512,256]{2,0,1:T(4,128)S(1)} fusion(f32[4,512,256]{2,0,1:T(4,128)S(1)} %fusion.4, f32[5,256,512]{1,0,2:T(8,128)} %copy.11, s32[5]{0:T(128)S(1)} %get-tuple-element.14), kind=kOutput, calls=%fused_computation.18 | convolution fusion | flops 31981588 | bytes 6815764 | tf_op jit(solution)/shard_map/tk,kxz->txz/dot_general | solution.py:48
  177.3 0.0 copy-start
  177.3 1.3 copy-done
  178.7 0.5 slice.89
  179.2 0.8 copy.22
  180.0 0.0 all-reduce.6.cloned.1.call-update
  180.1 0.0 all-gather.8.cloned.1.call-start
  180.1 31.8 %all-reduce.6.cloned.1.call-done = f32[512,256]{1,0:T(8,128)} async-done(((f32[512,256]{1,0:T(8,128)}), f32[512,256]{1,0:T(8,128)}) %all-reduce.6.cloned.1.call-update) | async-done | bytes 524304 | tf_op jit(solution)/shard_map/psum | solution.py:25
  211.9 2.4 convolution_convert_fusion.1
  214.3 0.0 all-gather.8.cloned.1.call-update
  214.3 0.2 all-reduce.8.cloned.1.call-start
  214.6 49.2 %all-gather.8.cloned.1.call-done = bf16[4096,256]{1,0:T(8,128)(2,1)} async-done(((bf16[512,256]{1,0:T(8,128)(2,1)}), bf16[4096,256]{1,0:T(8,128)(2,1)}) %all-gather.8.cloned.1.call-update) | async-done | bytes 2097168 | tf_op jit(solution)/shard_map/all_gather | solution.py:33
  263.8 1.1 dynamic-slice_bitcast_fusion
  264.8 1.8 gather_fusion.2
  266.6 3.2 fusion.6
  269.8 3.5 %copy.13 = f32[5,256,512]{1,0,2:T(8,128)} copy(f32[5,256,512]{2,1,0:T(8,128)S(1)} %fusion.6) | data formatting | bytes 5242880 | tf_op jit(solution)/shard_map/bij,bjr->bir/dot_general | solution.py:39
  273.3 4.2 %fusion = f32[4,512,256]{2,0,1:T(4,128)S(1)} fusion(f32[5,256,512]{1,0,2:T(8,128)} %copy.13, s32[5]{0:T(128)S(1)} %get-tuple-element.12), kind=kOutput, calls=%fused_computation.3 | convolution fusion | flops 31457300 | bytes 4718612 | tf_op jit(solution)/shard_map/tk,kxz->txz/dot_general | solution.py:48
  277.5 2.8 slice_add_fusion
  280.3 0.0 copy-start.1
  280.4 0.0 copy-start.2
  280.4 0.0 copy-start.3
  280.4 0.8 copy.21
  281.2 0.0 all-reduce.8.cloned.1.call-update
  281.2 31.9 %all-reduce.8.cloned.1.call-done = f32[512,256]{1,0:T(8,128)} async-done(((f32[512,256]{1,0:T(8,128)}), f32[512,256]{1,0:T(8,128)}) %all-reduce.8.cloned.1.call-update) | async-done | bytes 524304 | tf_op jit(solution)/shard_map/psum | solution.py:25
  313.1 1.7 fusion.24
  314.8 0.0 copy-done.1
  314.8 0.0 copy-done.2
  314.8 0.0 copy-done.3
  314.8 1.1 maximum_bitcast_fusion
  (3 shorter events, 0.0 us)
Async XLA Ops:
  6.5 55.0 %all-gather.4.cloned.1.call-start = ((), (), s32[]{:S(2)}) async-start(), calls=%async_computation | async-start | bytes 2359296 | tf_op jit(solution)/shard_map/all_gather | solution.py:33
  8.8 99.8 %all-reduce.4.cloned.1.call-start = ((), (), s32[]{:S(2)}) async-start(), calls=%async_computation.1 | async-start | bytes 1048576 | tf_op jit(solution)/shard_map/psum | solution.py:25
  76.7 83.7 %all-gather.6.cloned.1.call-start = ((), (), s32[]{:S(2)}) async-start(), calls=%async_computation.2 | async-start | bytes 2359296 | tf_op jit(solution)/shard_map/all_gather | solution.py:33
  110.9 101.0 %all-reduce.6.cloned.1.call-start = ((), (), s32[]{:S(2)}) async-start(), calls=%async_computation.3 | async-start | bytes 1048576 | tf_op jit(solution)/shard_map/psum | solution.py:25
  177.3 1.3 copy-start
  180.1 83.7 %all-gather.8.cloned.1.call-start = ((), (), s32[]{:S(2)}) async-start(), calls=%async_computation.4 | async-start | bytes 2359296 | tf_op jit(solution)/shard_map/all_gather | solution.py:33
  214.3 98.8 %all-reduce.8.cloned.1.call-start = ((), (), s32[]{:S(2)}) async-start(), calls=%async_computation.5 | async-start | bytes 1048576 | tf_op jit(solution)/shard_map/psum | solution.py:25
  280.3 34.4 %copy-start.1 = (bf16[512,256]{1,0:T(8,128)(2,1)S(1)}, bf16[512,256]{1,0:T(8,128)(2,1)}, u32[]{:S(2)}) copy-start(bf16[512,256]{1,0:T(8,128)(2,1)} %convolution_convert_fusion.3) | copy-start | bytes 786436
  280.4 34.4 %copy-start.2 = (bf16[256,512]{0,1:T(8,128)(2,1)S(1)}, bf16[256,512]{0,1:T(8,128)(2,1)}, u32[]{:S(2)}) copy-start(bf16[256,512]{0,1:T(8,128)(2,1)} %convolution_convert_fusion.2) | copy-start | bytes 786436
  280.4 34.4 %copy-start.3 = (bf16[256,512]{0,1:T(8,128)(2,1)S(1)}, bf16[256,512]{0,1:T(8,128)(2,1)}, u32[]{:S(2)}) copy-start(bf16[256,512]{0,1:T(8,128)(2,1)} %convolution_convert_fusion.1) | copy-start | bytes 786436
Sparse Core Ops, SparseCore 0:
  9.5 51.9 all-gather.3
  76.8 31.6 all-reduce.3
  111.0 49.2 all-gather.5
  180.2 31.6 all-reduce.5
  214.4 49.2 all-gather.7
  281.3 31.6 all-reduce.7
where the time goes:
time: 323 us
  waiting for transfers between devices  245 us (76%)
  matrix products  32.5 us (10%)
  local copies, waits for them, and re-layouts  26.2 us (8%)
  between operations  13.6 us (4%)
  other arithmetic  4.63 us (1%)
    all_gather x3, waiting for transfers between devices, on_device(): gathered = lax.all_gather(solved, 'prow', axis=0, tiled=True)  150 us
    psum x3, waiting for transfers between devices, on_device(): summed = lax.psum(partial_value[tree_level], 'pcol')  95.5 us
    dot_general x3, matrix products, on_device(): jnp.einsum('tk,kxz->txz', indicator_matrix, block_products, precision=lax...  12.8 us
    dot_general x3, local copies, waits for them, and re-layouts, on_device(): jnp.einsum('bij,bjr->bir', lower_blocks[0, 0, tree_level], picked, prefer...  12.1 us
    dot_general x3, matrix products, on_device(): jnp.einsum('bij,bjr->bir', lower_blocks[0, 0, tree_level], picked, prefer...  11 us
  transfers between devices with their start and end apart: 6, of which 6 were waited for; matrix products, arithmetic and copies ran while one was open for 0% of the time, Pallas kernels for 0%

commit v1 on v0

--- a/solution.py
+++ b/solution.py
@@ -22,7 +22,7 @@
                 inverse, given_rhs.astype(jnp.bfloat16), preferred_element_type=jnp.float32
             ).astype(jnp.bfloat16)
         else:
-            summed = lax.psum(partial_value[tree_level], "pcol")
+            summed = jnp.sum(lax.all_gather(partial_value[tree_level], "pcol"), axis=0)
             solved = jnp.dot(
                 inverse,
                 (given_rhs - summed).astype(jnp.bfloat16),

time: 323 us -> 296 us (0.916)
  waiting for transfers between devices: 245 us -> 214 us
  other arithmetic: 4.63 us -> 9.99 us
    psum x3 -> x0, waiting for transfers between devices: 95.5 us -> none  [on_device(): summed = lax.psum(partial_value[tree_level], 'pcol')]
    all_gather x0 -> x3, waiting for transfers between devices: none -> 63.6 us  [on_device(): summed = jnp.sum(lax.all_gather(partial_value[tree_level], 'pcol'), axis=0)]
    reduce_sum x0 -> x3, other arithmetic: none -> 5.36 us  [on_device(): summed = jnp.sum(lax.all_gather(partial_value[tree_level], 'pcol'), axis=0)]
where the time goes in v1:
time: 296 us
  waiting for transfers between devices  214 us (72%)
  matrix products  32 us (11%)
  local copies, waits for them, and re-layouts  26.2 us (9%)
  between operations  13.6 us (5%)
  other arithmetic  9.99 us (3%)
    all_gather x3, waiting for transfers between devices, on_device(): gathered = lax.all_gather(solved, 'prow', axis=0, tiled=True)  150 us
    all_gather x3, waiting for transfers between devices, on_device(): summed = jnp.sum(lax.all_gather(partial_value[tree_level], 'pcol'), axis=0)  63.6 us
    dot_general x3, matrix products, on_device(): jnp.einsum('tk,kxz->txz', indicator_matrix, block_products, precision=lax...  12.8 us
    dot_general x3, local copies, waits for them, and re-layouts, on_device(): jnp.einsum('bij,bjr->bir', lower_blocks[0, 0, tree_level], picked, prefer...  12.1 us
    dot_general x3, matrix products, on_device(): jnp.einsum('bij,bjr->bir', lower_blocks[0, 0, tree_level], picked, prefer...  11 us
    dot_general x3, matrix products, on_device(): jnp.dot(inverse, (given_rhs - summed).astype(jnp.bfloat16), preferred_ele...  5.96 us
  transfers between devices with their start and end apart: 6, of which 6 were waited for; matrix products, arithmetic and copies ran while one was open for 0% of the time, Pallas kernels for 0%

profile of v1, /device:TPU:0, one launch (start us, length us, event | category | flops | bytes accessed | tf_op | source)
XLA Modules:
  0.0 295.8 jit_solution(4617689639271186889)
XLA Ops:
  6.5 0.0 all-gather.7.cloned.1.call-start
  6.5 2.2 convolution_convert_fusion.3
  8.8 0.0 all-gather.7.cloned.1.call-update
  8.8 0.0 all-gather.9.cloned.1.call-start
  8.8 0.7 compare_and_fusion
  9.5 0.7 slice_bitcast_fusion
  10.2 51.3 %all-gather.7.cloned.1.call-done = bf16[4096,256]{1,0:T(8,128)(2,1)} async-done(((bf16[512,256]{1,0:T(8,128)(2,1)}), bf16[4096,256]{1,0:T(8,128)(2,1)}) %all-gather.7.cloned.1.call-update) | async-done | bytes 2097168 | tf_op jit(solution)/shard_map/all_gather | solution.py:33
  61.5 1.1 dynamic-slice_bitcast_fusion.2
  62.6 1.8 gather_fusion
  64.4 3.2 %fusion.10 = f32[5,256,512]{2,1,0:T(8,128)S(1)} fusion(bf16[1,1,3,5,512,512]{5,4,3,2,1,0:T(8,128)(2,1)} %param.9, bf16[5,512,256]{2,1,0:T(8,128)(2,1)} %gather_fusion, pred[5]{0:T(512)(128)(4,1)S(1)} %get-tuple-element.15), kind=kOutput, calls=%fused_computation.13 | convolution fusion | flops 671744000 | bytes 6553605 | tf_op jit(solution)/shard_map/bij,bjr->bir/dot_general | solution.py:39
  67.5 3.5 %copy.15 = f32[5,256,512]{1,0,2:T(8,128)} copy(f32[5,256,512]{2,1,0:T(8,128)S(1)} %fusion.10) | data formatting | bytes 5242880 | tf_op jit(solution)/shard_map/bij,bjr->bir/dot_general | solution.py:39
  71.0 4.2 %fusion.4 = f32[4,512,256]{2,0,1:T(4,128)S(1)} fusion(f32[5,256,512]{1,0,2:T(8,128)} %copy.15, s32[5]{0:T(128)S(1)} %get-tuple-element.13), kind=kOutput, calls=%fused_computation.7 | convolution fusion | flops 31457300 | bytes 4718612 | tf_op jit(solution)/shard_map/tk,kxz->txz/dot_general | solution.py:48
  75.3 0.5 slice.88
  75.8 0.8 copy.9
  76.7 0.0 all-gather.9.cloned.1.call-update
  76.7 0.0 all-gather.11.cloned.1.call-start
  76.7 21.2 %all-gather.9.cloned.1.call-done = f32[4,512,256]{2,1,0:T(8,128)} async-done(((f32[1,512,256]{2,1,0:T(8,128)}), f32[4,512,256]{2,1,0:T(8,128)}) %all-gather.9.cloned.1.call-update) | async-done | bytes 2097168 | tf_op jit(solution)/shard_map/all_gather | solution.py:25
  97.9 1.8 reduce_sum.33
  99.7 2.2 convolution_convert_fusion.2
  101.9 0.0 all-gather.11.cloned.1.call-update
  102.0 0.0 all-gather.13.cloned.1.call-start
  102.0 49.4 %all-gather.11.cloned.1.call-done = bf16[4096,256]{1,0:T(8,128)(2,1)} async-done(((bf16[512,256]{1,0:T(8,128)(2,1)}), bf16[4096,256]{1,0:T(8,128)(2,1)}) %all-gather.11.cloned.1.call-update) | async-done | bytes 2097168 | tf_op jit(solution)/shard_map/all_gather | solution.py:33
  151.4 1.1 dynamic-slice_bitcast_fusion.1
  152.5 1.8 gather_fusion.1
  154.2 4.7 %fusion.8 = f32[5,256,512]{2,1,0:T(8,128)} fusion(bf16[1,1,3,5,512,512]{5,4,3,2,1,0:T(8,128)(2,1)} %param.9, bf16[5,512,256]{2,1,0:T(8,128)(2,1)} %gather_fusion.1, pred[5]{0:T(512)(128)(4,1)S(1)} %get-tuple-element.17), kind=kOutput, calls=%fused_computation.11 | convolution fusion | flops 671744000 | bytes 6553605 | tf_op jit(solution)/shard_map/bij,bjr->bir/dot_general | solution.py:39
  158.9 5.0 %copy.17 = f32[5,256,512]{1,0,2:T(8,128)} copy(f32[5,256,512]{2,1,0:T(8,128)} %fusion.8) | data formatting | bytes 5242880 | tf_op jit(solution)/shard_map/bij,bjr->bir/dot_general | solution.py:39
  164.0 4.4 %fusion.15 = f32[4,512,256]{2,0,1:T(4,128)S(1)} fusion(f32[4,512,256]{2,0,1:T(4,128)S(1)} %fusion.4, f32[5,256,512]{1,0,2:T(8,128)} %copy.17, s32[5]{0:T(128)S(1)} %get-tuple-element.14), kind=kOutput, calls=%fused_computation.18 | convolution fusion | flops 31981588 | bytes 6815764 | tf_op jit(solution)/shard_map/tk,kxz->txz/dot_general | solution.py:48
  168.3 0.0 copy-start
  168.4 1.3 copy-done
  169.7 0.5 slice.89
  170.2 0.8 copy.11
  171.1 0.0 all-gather.13.cloned.1.call-update
  171.1 0.0 all-gather.15.cloned.1.call-start
  171.1 21.2 %all-gather.13.cloned.1.call-done = f32[4,512,256]{2,1,0:T(8,128)} async-done(((f32[1,512,256]{2,1,0:T(8,128)}), f32[4,512,256]{2,1,0:T(8,128)}) %all-gather.13.cloned.1.call-update) | async-done | bytes 2097168 | tf_op jit(solution)/shard_map/all_gather | solution.py:25
  192.3 1.8 reduce_sum.35
  194.1 2.2 convolution_convert_fusion.1
  196.3 0.0 all-gather.15.cloned.1.call-update
  196.4 0.2 all-gather.17.cloned.1.call-start
  196.6 49.2 %all-gather.15.cloned.1.call-done = bf16[4096,256]{1,0:T(8,128)(2,1)} async-done(((bf16[512,256]{1,0:T(8,128)(2,1)}), bf16[4096,256]{1,0:T(8,128)(2,1)}) %all-gather.15.cloned.1.call-update) | async-done | bytes 2097168 | tf_op jit(solution)/shard_map/all_gather | solution.py:33
  245.8 1.1 dynamic-slice_bitcast_fusion
  246.9 1.8 gather_fusion.2
  248.7 3.2 %fusion.6 = f32[5,256,512]{2,1,0:T(8,128)S(1)} fusion(bf16[1,1,3,5,512,512]{5,4,3,2,1,0:T(8,128)(2,1)} %param.9, bf16[5,512,256]{2,1,0:T(8,128)(2,1)} %gather_fusion.2, pred[5]{0:T(512)(128)(4,1)S(1)} %get-tuple-element.6), kind=kOutput, calls=%fused_computation.9 | convolution fusion | flops 671744000 | bytes 6553605 | tf_op jit(solution)/shard_map/bij,bjr->bir/dot_general | solution.py:39
  251.8 3.5 %copy.19 = f32[5,256,512]{1,0,2:T(8,128)} copy(f32[5,256,512]{2,1,0:T(8,128)S(1)} %fusion.6) | data formatting | bytes 5242880 | tf_op jit(solution)/shard_map/bij,bjr->bir/dot_general | solution.py:39
  255.3 4.2 %fusion = f32[4,512,256]{2,0,1:T(4,128)S(1)} fusion(f32[5,256,512]{1,0,2:T(8,128)} %copy.19, s32[5]{0:T(128)S(1)} %get-tuple-element.12), kind=kOutput, calls=%fused_computation.3 | convolution fusion | flops 31457300 | bytes 4718612 | tf_op jit(solution)/shard_map/tk,kxz->txz/dot_general | solution.py:48
  259.6 2.8 slice_add_fusion
  262.4 0.8 copy.13
  263.2 0.0 all-gather.17.cloned.1.call-update
  263.2 0.0 copy-start.1
  263.2 0.0 copy-start.2
  263.2 0.0 copy-start.3
  263.3 21.2 %all-gather.17.cloned.1.call-done = f32[4,512,256]{2,1,0:T(8,128)} async-done(((f32[1,512,256]{2,1,0:T(8,128)}), f32[4,512,256]{2,1,0:T(8,128)}) %all-gather.17.cloned.1.call-update) | async-done | bytes 2097168 | tf_op jit(solution)/shard_map/all_gather | solution.py:25
  284.5 1.8 reduce_sum.37
  286.3 1.5 fusion.24
  287.8 0.0 copy-done.1
  287.8 0.0 copy-done.2
  287.8 0.0 copy-done.3
  287.8 1.1 maximum_bitcast_fusion
  (3 shorter events, 0.0 us)
Async XLA Ops:
  6.5 55.0 %all-gather.7.cloned.1.call-start = ((), (), s32[]{:S(2)}) async-start(), calls=%async_computation | async-start | bytes 2359296 | tf_op jit(solution)/shard_map/all_gather | solution.py:33
  8.8 89.1 %all-gather.9.cloned.1.call-start = ((), (), s32[]{:S(2)}) async-start(), calls=%async_computation.1 | async-start | bytes 2621440 | tf_op jit(solution)/shard_map/all_gather | solution.py:25
  76.7 74.7 %all-gather.11.cloned.1.call-start = ((), (), s32[]{:S(2)}) async-start(), calls=%async_computation.2 | async-start | bytes 2359296 | tf_op jit(solution)/shard_map/all_gather | solution.py:33
  102.0 90.4 %all-gather.13.cloned.1.call-start = ((), (), s32[]{:S(2)}) async-start(), calls=%async_computation.3 | async-start | bytes 2621440 | tf_op jit(solution)/shard_map/all_gather | solution.py:25
  168.3 1.3 copy-start
  171.1 74.7 %all-gather.15.cloned.1.call-start = ((), (), s32[]{:S(2)}) async-start(), calls=%async_computation.4 | async-start | bytes 2359296 | tf_op jit(solution)/shard_map/all_gather | solution.py:33
  196.4 88.1 %all-gather.17.cloned.1.call-start = ((), (), s32[]{:S(2)}) async-start(), calls=%async_computation.5 | async-start | bytes 2621440 | tf_op jit(solution)/shard_map/all_gather | solution.py:25
  263.2 24.6 %copy-start.1 = (bf16[512,256]{1,0:T(8,128)(2,1)S(1)}, bf16[512,256]{1,0:T(8,128)(2,1)}, u32[]{:S(2)}) copy-start(bf16[512,256]{1,0:T(8,128)(2,1)} %convolution_convert_fusion.3) | copy-start | bytes 786436
  263.2 24.6 %copy-start.2 = (bf16[256,512]{0,1:T(8,128)(2,1)S(1)}, bf16[256,512]{0,1:T(8,128)(2,1)}, u32[]{:S(2)}) copy-start(bf16[256,512]{0,1:T(8,128)(2,1)} %convolution_convert_fusion.2) | copy-start | bytes 786436
  263.2 24.6 %copy-start.3 = (bf16[256,512]{0,1:T(8,128)(2,1)S(1)}, bf16[256,512]{0,1:T(8,128)(2,1)}, u32[]{:S(2)}) copy-start(bf16[256,512]{0,1:T(8,128)(2,1)} %convolution_convert_fusion.1) | copy-start | bytes 786436
Sparse Core Ops, SparseCore 0:
  9.5 51.9 all-gather.6
  76.8 21.0 all-gather.8
  102.1 49.2 all-gather.10
  171.2 21.0 all-gather.12
  196.5 49.2 all-gather.14
  263.4 21.0 all-gather.16
